TPU v7x, 512 devices: a whole 4x4x16 slice. The times are simulated.
512 devices in a mesh: replica: 32 (over z, y_lo), fsdp: 16 (over x, y_hi, core).
Axes of the slice: x: 4, y: 4 (y_hi: 2, y_lo: 2; y = y_hi * 2 + y_lo), z: 16, core: 2. Of those that a mesh axis runs over, the one named last changes fastest.
Arguments:
- residual: bfloat16 [32, 2048, 2560], P('replica', 'fsdp'), may hold values from -6 to 6
- attention: bfloat16 [32, 2048, 2560], P('replica', 'fsdp'), may hold values from -6 to 6
- out_weight: bfloat16 [32, 2560, 2560], P('replica', None, 'fsdp'), may hold values from -6 to 6
- norm_gain: bfloat16 [32, 2560], P('replica', 'fsdp'), may hold values from 0.5 to 1.5
- cotangent: bfloat16 [32, 2048, 2560], P('replica', 'fsdp'), may hold values from -6 to 6
- step_index: int32 [1], replicated, may hold values from 0 to 63
Outputs:
- normed_out: bfloat16 [32, 2048, 2560], P('replica', 'fsdp')
- grad_residual: bfloat16 [32, 2048, 2560], P('replica', 'fsdp')
- mixed_weight: bfloat16 [32, 2560, 2560], P('replica', None, 'fsdp')
- mixed_gain: bfloat16 [32, 2560], P('replica', 'fsdp')
All inputs are finite; a program needn't handle non-finite values.
Results may differ from a plain program's by a relative error of at most 0.0052.
Values may be sent and summed in bfloat16 or wider, within the bound.
A program may use at most 64 MiB of HBM per device.

v0:
```python
from functools import partial
import math

import jax
import jax.numpy as jnp
from jax import lax
from jax.sharding import PartitionSpec as P

epsilon = 1e-05
rate_weight = 0.2
rate_gain = 0.005


def shortened(value):

    def short(part):
        return part.astype(jnp.bfloat16) if part.dtype == jnp.float32 else part

    return jax.tree.map(short, value)


def passed_along(block, axis, distance):
    devices = range(lax.axis_size(axis))
    route = [((i - distance) % len(devices), i) for i in devices]
    return lax.ppermute(block, axis, route)


def shift_update(payload, distance):
    return jax.tree.map(
        lambda part, own: part.astype(own.dtype),
        passed_along(shortened(payload), "replica", distance),
        payload,
    )


def from_partner(mover, payload, step_index, hop_count):
    branches = [partial(mover, distance=2**level) for level in range(hop_count)]
    branch_index = step_index[0] % hop_count
    return lax.switch(branch_index, branches, payload)


def body(residual, attention, out_weight, norm_gain, cotangent, step_index):
    local_heads = attention[0]
    weight_local = out_weight[0]
    gain_local = norm_gain[0]
    col_count = weight_local.shape[1]
    factor = 1.0 / math.sqrt(local_heads.shape[1])
    hop_count = lax.axis_size("replica").bit_length() - 1
    gathered = lax.all_gather(local_heads, "fsdp", axis=0, tiled=True)
    projected = jnp.dot(gathered, weight_local, preferred_element_type=jnp.float32) * factor
    proj_cols = projected.astype(jnp.bfloat16)
    tok_proj = lax.all_to_all(proj_cols, "fsdp", split_axis=0, concat_axis=1, tiled=True)
    gain_every = lax.all_gather(gain_local, "fsdp", axis=0, tiled=True).astype(jnp.float32)
    summed = residual[0].astype(jnp.float32) + tok_proj.astype(jnp.float32)
    inv_rms = lax.rsqrt(jnp.mean(summed * summed, axis=-1, keepdims=True) + epsilon)
    normed = summed * inv_rms
    normed_out = (normed * gain_every).astype(jnp.bfloat16)
    cot_full = cotangent[0].astype(jnp.float32)
    grad_normed = cot_full * gain_every
    inner_mean = jnp.mean(grad_normed * normed, axis=-1, keepdims=True)
    grad_res = ((grad_normed - normed * inner_mean) * inv_rms).astype(jnp.bfloat16)
    col_start = lax.axis_index("fsdp") * col_count
    partial_gain = jnp.sum(cot_full * normed, axis=0)
    gain_totals = lax.psum(partial_gain, "fsdp")
    grad_gain = lax.dynamic_slice_in_dim(gain_totals, col_start, col_count, 0)
    grad_columns = lax.all_to_all(grad_res, "fsdp", split_axis=1, concat_axis=0, tiled=True)
    grad_weight = (
        lax.dot_general(
            gathered, grad_columns, (((0,), (0,)), ((), ())), preferred_element_type=jnp.float32
        )
        * factor
    )
    new_weight = (weight_local.astype(jnp.float32) - rate_weight * grad_weight).astype(jnp.bfloat16)
    new_gain = (gain_local.astype(jnp.float32) - rate_gain * grad_gain).astype(jnp.bfloat16)
    other_weight, other_gain = from_partner(
        shift_update, (new_weight, new_gain), step_index, hop_count
    )
    mixed_weight = (
        0.5 * (new_weight.astype(jnp.float32) + other_weight.astype(jnp.float32))
    ).astype(jnp.bfloat16)
    mixed_gain = (0.5 * (new_gain.astype(jnp.float32) + other_gain.astype(jnp.float32))).astype(
        jnp.bfloat16
    )
    return (normed_out[None], grad_res[None], mixed_weight[None], mixed_gain[None])


def solution(mesh):
    return jax.shard_map(
        body,
        mesh=mesh,
        in_specs=(
            P("replica", "fsdp", None),
            P("replica", "fsdp", None),
            P("replica", None, "fsdp"),
            P("replica", "fsdp"),
            P("replica", "fsdp", None),
            P(),
        ),
        out_specs=(
            P("replica", "fsdp", None),
            P("replica", "fsdp", None),
            P("replica", None, "fsdp"),
            P("replica", "fsdp"),
        ),
        check_vma=False,
    )
```

profile of v0, /device:TPU:160, one launch (start us, length us, event | category | flops | bytes accessed | tf_op | source)
XLA Modules:
  0.0 340.1 jit_solution(346781242679851186)
XLA Ops:
  7.2 0.0 all-gather.4.cloned.1.call-start
  7.2 0.7 all-gather.4.cloned.1.call-update
  7.9 102.9 %all-gather.4.cloned.1.call-done = bf16[1,2048,2560]{2,1,0:T(8,128)(2,1)} async-done(((bf16[1,128,2560]{2,1,0:T(8,128)(2,1)}), bf16[1,2048,2560]{2,1,0:T(8,128)(2,1)}) %all-gather.4.cloned.1.call-update) | async-done | bytes 10485776 | tf_op jit(solution)/shard_map/all_gather | solution.py:49
  110.8 7.7 %fusion.33 = bf16[20,16,8,128]{3,2,1,0:T(8,128)(2,1)S(1)} fusion(bf16[1,2048,2560]{2,1,0:T(8,128)(2,1)} %all-gather.4.cloned.1.call-done, bf16[1,2560,160]{1,2,0:T(8,128)(2,1)} %param.13), kind=kOutput, calls=%fused_computation.30 | convolution fusion | flops 1678376960 | bytes 11960320 | tf_op jit(solution)/shard_map/dot_general | solution.py:50
  118.5 0.0 copy-start.2
  118.5 0.0 copy-start
  118.5 0.9 copy.56
  119.5 0.0 copy-start.1
  119.5 3.7 %all-to-all-start = ((bf16[16,128,160]{1,2,0:T(8,128)(2,1)}), bf16[16,128,160]{1,2,0:T(8,128)(2,1)S(1)}, u32[]{:S(2)}, u32[]{:S(2)}) async-start(bf16[16,128,160]{1,2,0:T(8,128)(2,1)} %bitcast.97), calls=%async_computation | async-start | bytes 1310720 | tf_op jit(solution)/shard_map/all_to_all | solution.py:52
  123.9 1.3 dynamic-slice
  125.8 0.0 copy-done.2
  125.9 0.2 dynamic-update-slice
  126.1 38.9 %all-reduce = bf16[2560]{0:T(1024)(128)(2,1)S(1)} all-reduce(bf16[2560]{0:T(1024)(128)(2,1)S(1)} %dynamic-update-slice), channel_id=3, replica_groups=mesh['replica'=32,'fsdp'=16] {'fsdp'}, use_global_device_ids=true, to_apply=%add | all-reduce | flops 2560 | bytes 10240
  165.0 0.1 mul.133
  165.1 0.0 copy-done
  165.1 0.3 copy.43
  165.4 0.0 copy-done.1
  165.5 0.3 copy.45
  165.8 0.0 all-to-all-done
  165.8 0.4 multiply_reduce_fusion
  166.2 0.8 fusion.27
  167.0 1.4 fusion.32
  168.4 3.6 %all-to-all-start.1 = ((bf16[128,16,160]{0,2,1:T(8,128)(2,1)}), bf16[128,16,160]{0,2,1:T(8,128)(2,1)S(1)}, u32[]{:S(2)}, u32[]{:S(2)}) async-start(bf16[128,16,160]{0,2,1:T(8,128)(2,1)} %fusion.32), calls=%async_computation.1 | async-start | bytes 1310720 | tf_op jit(solution)/shard_map/all_to_all | solution.py:66
  172.0 0.1 convert_element_type.177
  172.1 0.5 multiply_convert_fusion
  172.6 1.1 copy.48
  173.7 0.0 copy-start.3
  173.7 1.1 copy.47
  174.8 70.0 %psum.7 = f32[2560]{0:T(1024)S(1)} all-reduce(f32[2560]{0:T(1024)S(1)} %get-tuple-element.98), channel_id=1, replica_groups=mesh['replica'=32,'fsdp'=16] {'fsdp'}, use_global_device_ids=true, to_apply=%region_3.0 | all-reduce | flops 2560 | bytes 20480 | tf_op jit(solution)/shard_map/psum | solution.py:64
  244.9 0.1 subtract_convert_fusion
  245.0 0.0 all-to-all-done.1
  245.0 0.0 copy-done.3
  245.0 5.9 %fusion.13 = bf16[2560,160]{0,1:T(8,128)(2,1)S(1)} fusion(bf16[1,2048,2560]{2,1,0:T(8,128)(2,1)} %all-gather.4.cloned.1.call-done, bf16[1,2560,160]{1,2,0:T(8,128)(2,1)S(1)} %copy-done.3, bf16[128,16,160]{0,2,1:T(8,128)(2,1)S(1)} %all-to-all-done.1), kind=kOutput, calls=%fused_computation.7 | convolution fusion | flops 1679360000 | bytes 12779520 | tf_op jit(solution)/shard_map/dot_general | solution.py:68
  250.9 78.9 %conditional.4 = (bf16[2560,160]{0,1:T(8,128)(2,1)}, bf16[160]{0:T(256)(128)(2,1)}) conditional(s32[]{:T(128)} %clamp.3, (bf16[2560,160]{0,1:T(8,128)(2,1)S(1)}, bf16[160]{0:T(256)(128)(2,1)S(1)}) %tuple.60, (bf16[2560,160]{0,1:T(8,128)(2,1)S(1)}, bf16[160]{0:T(256)(128)(2,1)S(1)}) %tuple.60, ...), branch_computations={%region_4.5_spmd, %region_5.6_spmd, %region_6.7_spmd, %region_7.8_... | conditional | bytes 3278176
  250.9 7.1 %collective-permute-start.8 = (bf16[2560,160]{0,1:T(8,128)(2,1)S(1)}, bf16[2560,160]{0,1:T(8,128)(2,1)}, u32[]{:S(2)}, u32[]{:S(2)}) collective-permute-start(bf16[2560,160]{0,1:T(8,128)(2,1)S(1)} %get-tuple-element.40), channel_id=1, source_target_pairs={{256,0},{272,16},{288,32},{304,48},{320,64},{336,80},{352,96},{368... | collective-permute-start | bytes 2457608 | tf_op jit(solution)/shard_map/cond/branch_4_fun/ppermute | solution.py:25
  258.1 7.4 %collective-permute-start.9 = (bf16[160]{0:T(256)(128)(2,1)S(1)}, bf16[160]{0:T(256)(128)(2,1)}, u32[]{:S(2)}, u32[]{:S(2)}) collective-permute-start(bf16[160]{0:T(256)(128)(2,1)S(1)} %get-tuple-element.41), channel_id=1, source_target_pairs={{256,0},{272,16},{288,32},{304,48},{320,64},{336,80},{352,96},{368... | collective-permute-start | bytes 968 | tf_op jit(solution)/shard_map/cond/branch_4_fun/ppermute | solution.py:25
  265.5 64.3 %collective-permute-done.9 = bf16[160]{0:T(256)(128)(2,1)} collective-permute-done((bf16[160]{0:T(256)(128)(2,1)S(1)}, bf16[160]{0:T(256)(128)(2,1)}, u32[]{:S(2)}, u32[]{:S(2)}) %collective-permute-start.9) | collective-permute-done | bytes 352 | tf_op jit(solution)/shard_map/cond/branch_4_fun/ppermute | solution.py:25
  329.8 0.0 collective-permute-done.8
  329.8 0.6 fusion.41
  330.4 2.3 fusion.36
  332.7 0.6 broadcast_in_dim.5
  (5 shorter events, 0.0 us)
Async XLA Ops:
  7.2 103.7 %all-gather.4.cloned.1.call-start = ((), (), s32[]{:S(2)}) async-start(), calls=%async_computation.2 | async-start | bytes 11141120 | tf_op jit(solution)/shard_map/all_gather | solution.py:49
  118.5 7.3 %copy-start.2 = (bf16[1,160]{1,0:T(2,128)(2,1)S(1)}, bf16[1,160]{1,0:T(2,128)(2,1)}, u32[]{:S(2)}) copy-start(bf16[1,160]{1,0:T(2,128)(2,1)} %param.14) | copy-start | bytes 964
  118.5 46.6 %copy-start = (bf16[1,128,2560]{2,1,0:T(8,128)(2,1)S(1)}, bf16[1,128,2560]{2,1,0:T(8,128)(2,1)}, u32[]{:S(2)}) copy-start(bf16[1,128,2560]{2,1,0:T(8,128)(2,1)} %param.11) | copy-start | bytes 1966084
  119.5 46.0 %copy-start.1 = (bf16[1,128,2560]{2,1,0:T(8,128)(2,1)S(1)}, bf16[1,128,2560]{2,1,0:T(8,128)(2,1)}, u32[]{:S(2)}) copy-start(bf16[1,128,2560]{2,1,0:T(8,128)(2,1)} %param.15) | copy-start | bytes 1966084
  119.5 46.3 %all-to-all-start = ((bf16[16,128,160]{1,2,0:T(8,128)(2,1)}), bf16[16,128,160]{1,2,0:T(8,128)(2,1)S(1)}, u32[]{:S(2)}, u32[]{:S(2)}) async-start(bf16[16,128,160]{1,2,0:T(8,128)(2,1)} %bitcast.97), calls=%async_computation | async-start | bytes 1310720 | tf_op jit(solution)/shard_map/all_to_all | solution.py:52
  168.4 76.6 %all-to-all-start.1 = ((bf16[128,16,160]{0,2,1:T(8,128)(2,1)}), bf16[128,16,160]{0,2,1:T(8,128)(2,1)S(1)}, u32[]{:S(2)}, u32[]{:S(2)}) async-start(bf16[128,16,160]{0,2,1:T(8,128)(2,1)} %fusion.32), calls=%async_computation.1 | async-start | bytes 1310720 | tf_op jit(solution)/shard_map/all_to_all | solution.py:66
  173.7 71.2 %copy-start.3 = (bf16[1,2560,160]{1,2,0:T(8,128)(2,1)S(1)}, bf16[1,2560,160]{1,2,0:T(8,128)(2,1)}, u32[]{:S(2)}) copy-start(bf16[1,2560,160]{1,2,0:T(8,128)(2,1)} %param.13) | copy-start | bytes 2457604
  250.9 78.8 %collective-permute-start.8 = (bf16[2560,160]{0,1:T(8,128)(2,1)S(1)}, bf16[2560,160]{0,1:T(8,128)(2,1)}, u32[]{:S(2)}, u32[]{:S(2)}) collective-permute-start(bf16[2560,160]{0,1:T(8,128)(2,1)S(1)} %get-tuple-element.40), channel_id=1, source_target_pairs={{256,0},{272,16},{288,32},{304,48},{320,64},{336,80},{352,96},{368... | collective-permute-start | bytes 2457608 | tf_op jit(solution)/shard_map/cond/branch_4_fun/ppermute | solution.py:25
  258.1 71.7 %collective-permute-start.9 = (bf16[160]{0:T(256)(128)(2,1)S(1)}, bf16[160]{0:T(256)(128)(2,1)}, u32[]{:S(2)}, u32[]{:S(2)}) collective-permute-start(bf16[160]{0:T(256)(128)(2,1)S(1)} %get-tuple-element.41), channel_id=1, source_target_pairs={{256,0},{272,16},{288,32},{304,48},{320,64},{336,80},{352,96},{368... | collective-permute-start | bytes 968 | tf_op jit(solution)/shard_map/cond/branch_4_fun/ppermute | solution.py:25
Sparse Core Ops, SparseCore 0:
  11.3 99.5 all-gather.3
where the time goes:
time: 341 us; the launch traced here: 340 us
  waiting for transfers between devices  168 us (49%)
  blocking collectives  109 us (32%)
  starting transfers between devices  21.9 us (6%)
  between operations  15.5 us (5%)
  matrix products  13.6 us (4%)
  other arithmetic  6.22 us (2%)
  local copies, waits for them, and re-layouts  5.98 us (2%)
    all_gather x1, waiting for transfers between devices, body(): gathered = lax.all_gather(local_heads, 'fsdp', axis=0, tiled=True)  103 us
    psum x1, blocking collectives, body(): gain_totals = lax.psum(partial_gain, 'fsdp')  70 us
    ppermute x2, waiting for transfers between devices, passed_along(): return lax.ppermute(block, axis, route)  64.3 us
    unnamed x1, blocking collectives  38.9 us
    ppermute x2, starting transfers between devices, passed_along(): return lax.ppermute(block, axis, route)  14.6 us
    dot_general x1, matrix products, body(): jnp.dot(gathered, weight_local, preferred_element_type=jnp.float32) * factor  7.66 us
  transfers between devices with their start and end apart: 5, of which 2 were waited for; matrix products, arithmetic and copies ran while one was open for 2% of the time, Pallas kernels for 0%

commit v1 on v0

v1 whole, which is shorter than its diff:
```python
from functools import partial
import math

import jax
import jax.numpy as jnp
from jax import lax
from jax.experimental import pallas as pl
from jax.experimental.pallas import tpu as pltpu
from jax.sharding import PartitionSpec as P

EPSILON = 1e-05
RATE_WEIGHT = 0.2
RATE_GAIN = 0.005
MESH = pl.DeviceIdType.MESH
F32 = jnp.float32
BF16 = jnp.bfloat16

D = 2560
T = 128
C = 160
Q = 640
LANES = 128
CHUNK = 512
NCH = D // CHUNK


def kernel(
    distance,
    att, res, cot, weight, gain,
    normed_out, grad_out, mixed_out, mixed_gain_out,
    a, wbuf, wt, rbuf, cbuf, res_t, gn_t, pts, ptr, gts, gt, nbuf, gbuf,
    ysend, yrecv, own, new, other, mixed,
    gplace, gquad, gall, pg, pgx, pgs, pgq, ngain, ogain, mgain,
    load_sem, out_sem,
    a_send, a_recv, sib_send, sib_recv, w_send, w_recv,
    g1_send, g1_recv, g2_send, g2_recv,
    p_send, p_recv, t_send, t_recv, s1_send, s1_recv, s2_send, s2_recv,
    y_send, y_recv, z_send, z_recv, zg_send, zg_recv,
):
    r = lax.axis_index("replica")
    f = lax.axis_index("fsdp")
    replicas = lax.axis_size("replica")
    x, y, c = f // 4, (f // 2) % 2, f % 2
    s = x * 2 + c
    factor = 1.0 / math.sqrt(D)

    def at(px, py, pc, pr=r):
        return (pr, px * 4 + py * 2 + pc)

    def rx(step):
        return (x + step) % 4

    def send(src, dst, ss, rs, target):
        cp = pltpu.make_async_remote_copy(
            src_ref=src, dst_ref=dst, send_sem=ss, recv_sem=rs, device_id=target, device_id_type=MESH
        )
        cp.start()
        return cp

    def got(ref, ss, rs):
        pltpu.make_async_remote_copy(
            src_ref=ref, dst_ref=ref, send_sem=ss, recv_sem=rs, device_id=at(rx(1), y, c), device_id_type=MESH
        ).wait_recv()

    sends = []

    def rows(slot, start=0, size=T):
        return pl.ds(pl.multiple_of(slot * T + start, 64), size)

    load_a = pltpu.make_async_copy(att, a.at[rows(s)], load_sem.at[0])
    load_w = pltpu.make_async_copy(weight, wbuf, load_sem.at[1])
    load_r = pltpu.make_async_copy(res, rbuf, load_sem.at[2])
    load_c = pltpu.make_async_copy(cot, cbuf, load_sem.at[3])
    load_g = pltpu.make_async_copy(gain, gplace, load_sem.at[4])
    for cp in (load_a, load_w, load_g, load_r, load_c):
        cp.start()

    dst_r = (r + distance) % replicas
    src_r = (r + replicas - distance) % replicas
    peers = [at(rx(k), y, c) for k in (1, 2, 3)] + [at(rx(k), y, 1 - c) for k in range(4)]
    peers += [at(x, 1 - y, c), at(x, 1 - y, 1 - c), at(x, y, c, dst_r)]
    if 2 * distance != replicas:
        peers.append(at(x, y, c, src_r))
    barrier = pltpu.get_barrier_semaphore()
    for peer in peers:
        pl.semaphore_signal(barrier, inc=1, device_id=peer, device_id_type=MESH)
    load_a.wait()
    pl.semaphore_wait(barrier, len(peers))

    left, right, far = rx(3), rx(1), rx(2)
    for h in (0, 1):
        span = rows(s, 64 * h, 64)
        sends.append(send(a.at[span], a.at[span], a_send.at[0, h], a_recv.at[0, h], at(right, y, c)))
        h2 = 1 - h
        span = rows(s, 64 * h2, 64)
        sends.append(send(a.at[span], a.at[span], a_send.at[1, h2], a_recv.at[1, h2], at(left, y, c)))
    sends.append(send(a.at[rows(s)], a.at[rows(s)], sib_send.at[0], sib_recv.at[0], at(x, y, 1 - c)))

    load_w.wait()
    my_rows = pl.multiple_of(y * C, 32)
    peer_rows = pl.multiple_of((1 - y) * C, 32)

    def turn(k, _):
        k0 = pl.multiple_of(k * LANES, LANES)
        wt[pl.ds(my_rows, C), pl.ds(k0, LANES)] = wbuf[pl.ds(k0, LANES), :].T
        return 0

    lax.fori_loop(0, D // LANES, turn, 0)
    for h in (0, 1):
        span = pl.ds(pl.multiple_of(y * C + 80 * h, 16), 80)
        sends.append(send(wt.at[span], wt.at[span], w_send.at[h], w_recv.at[h], at(x, 1 - y, c)))

    load_g.wait()
    gquad[0] = gplace[...]
    quad = [at(x, y, 1 - c), at(x, 1 - y, c), at(x, 1 - y, 1 - c)]
    for i, peer in enumerate(quad):
        sends.append(send(gplace, gquad.at[1 + i], g1_send.at[i], g1_recv.at[i], peer))

    load_r.wait()
    load_c.wait()

    def turn_res(k, _):
        k0 = pl.multiple_of(k * LANES, LANES)
        res_t[pl.ds(k0, LANES), :] = rbuf[:, pl.ds(k0, LANES)].T
        return 0

    lax.fori_loop(0, D // LANES, turn_res, 0)

    for i in range(3):
        got(gquad.at[1 + i], g1_send.at[i], g1_recv.at[i])
    gall[x] = gquad[0] + gquad[1] + gquad[2] + gquad[3]
    for i, k in enumerate((1, 2, 3)):
        sends.append(send(gall.at[x], gall.at[x], g2_send.at[i], g2_recv.at[i], at(rx(k), y, c)))

    def projected(px, wrow):
        tokens = a[pl.ds(pl.multiple_of(px * 256, 256), 256), :]
        out = lax.dot_general(
            wt[pl.ds(wrow, C), :], tokens, (((1,), (1,)), ((), ())), preferred_element_type=F32
        )
        out = (out * factor).astype(BF16)
        for k in (0, 1):
            pts[px, k, pl.ds(wrow, C), :] = out[:, k * T : (k + 1) * T]

    def feature_rows(px, py, pc):
        return pl.ds(pl.multiple_of(px * Q + py * 2 * C + pc * C, 32), C)

    def hand_out(step, px, wrow, wy, i):
        for k in (0, 1):
            span = feature_rows(x, wy, c)
            src = pts.at[px, k, pl.ds(wrow, C), :]
            pc = c if k == 0 else 1 - c
            src = pts.at[px, pc, pl.ds(wrow, C), :]
            if step == 0 and k == 0:
                ptr[span, :] = src[...]
            else:
                sends.append(
                    send(src, ptr.at[span], p_send.at[step, k, i], p_recv.at[s, i], at(px, y, pc))
                )

    got(a.at[rows(x * 2 + 1 - c)], sib_send.at[0], sib_recv.at[0])
    projected(x, my_rows)
    hand_out(0, x, my_rows, y, 0)

    def forward(slot, h, i):
        span = rows(slot, 64 * h, 64)
        sends.append(send(a.at[span], a.at[span], sib_send.at[i], sib_recv.at[i], at(x, y, 1 - c)))

    def pass_on(slot, h, d, target):
        span = rows(slot, 64 * h, 64)
        sends.append(send(a.at[span], a.at[span], a_send.at[2, d], a_recv.at[2, d], target))

    got(a.at[rows(left * 2 + c, 0, 64)], a_send.at[0, 0], a_recv.at[0, 0])
    pass_on(left * 2 + c, 0, 0, at(right, y, c))
    got(a.at[rows(right * 2 + c, 64, 64)], a_send.at[1, 1], a_recv.at[1, 1])
    pass_on(right * 2 + c, 1, 1, at(left, y, c))
    forward(left * 2 + c, 0, 1)
    forward(right * 2 + c, 1, 4)

    for i, k in enumerate((3, 2, 1)):
        got(gall.at[rx(k)], g2_send.at[i], g2_recv.at[i])
    for px in range(4):
        for k in range(Q // LANES):
            k0 = px * Q + k * LANES
            row = gall[px, 0:1, k * LANES : (k + 1) * LANES].astype(F32)
            gn_t[k0 : k0 + LANES, :] = (cbuf[:, k0 : k0 + LANES].astype(F32) * row).T

    got(a.at[rows(left * 2 + c, 64, 64)], a_send.at[0, 1], a_recv.at[0, 1])
    forward(left * 2 + c, 1, 2)
    got(a.at[rows(right * 2 + c, 0, 64)], a_send.at[1, 0], a_recv.at[1, 0])
    forward(right * 2 + c, 0, 3)
    sib = 1 - c
    for h in (0, 1):
        got(a.at[rows(left * 2 + sib, 64 * h, 64)], sib_send.at[1 + h], sib_recv.at[1 + h])
    projected(left, my_rows)
    hand_out(1, left, my_rows, y, 0)
    for h in (0, 1):
        got(a.at[rows(right * 2 + sib, 64 * h, 64)], sib_send.at[3 + h], sib_recv.at[3 + h])
    projected(right, my_rows)
    hand_out(2, right, my_rows, y, 0)

    for h in (0, 1):
        span = pl.ds(pl.multiple_of((1 - y) * C + 80 * h, 16), 80)
        got(wt.at[span], w_send.at[h], w_recv.at[h])
    for step, px in ((1, left), (2, right), (0, x)):
        projected(px, peer_rows)
        hand_out(step, px, peer_rows, 1 - y, 1)
    for h in (0, 1):
        got(a.at[rows(far * 2 + c, 64 * h, 64)], a_send.at[2, h], a_recv.at[2, h])
        forward(far * 2 + c, h, 5 + h)
    for h in (0, 1):
        got(a.at[rows(far * 2 + sib, 64 * h, 64)], sib_send.at[5 + h], sib_recv.at[5 + h])
    projected(far, my_rows)
    hand_out(3, far, my_rows, y, 0)
    projected(far, peer_rows)
    hand_out(3, far, peer_rows, 1 - y, 1)

    for k in (0, 1):
        for step in range(4):
            if k == 0 and step == 0:
                continue
            px, pc = rx(step), (c if k == 0 else 1 - c)
            for i in (0, 1):
                py = y if i == 0 else 1 - y
                got(ptr.at[feature_rows(px, py, pc)], p_send.at[step, k, i], p_recv.at[px * 2 + pc, i])

    def folded(v):
        return v.reshape(LANES // 8, 8, T).sum(axis=0)

    def stats(k, carry):
        ss, gs = carry
        span = pl.ds(pl.multiple_of(k * LANES, LANES), LANES)
        sm = res_t[span, :].astype(F32) + ptr[span, :].astype(F32)
        return ss + folded(sm * sm), gs + folded(sm * gn_t[span, :])

    zero = jnp.zeros((8, T), F32)
    ss, gs = lax.fori_loop(0, D // LANES, stats, (zero, zero))
    inv = lax.rsqrt(ss.sum(axis=0, keepdims=True) * (1.0 / D) + EPSILON)
    inner = gs.sum(axis=0, keepdims=True) * (1.0 / D) * inv
    pull = inner * inv * inv

    for step in (2, 1, 3, 0):
        px = rx(step)

        def grads(k, _):
            span = pl.ds(pl.multiple_of(px * Q + k * LANES, LANES), LANES)
            sm = res_t[span, :].astype(F32) + ptr[span, :].astype(F32)
            gts[span, :] = (gn_t[span, :] * inv - sm * pull).astype(BF16)
            return 0

        lax.fori_loop(0, Q // LANES, grads, 0)
        for k in (0, 1):
            pc = c if k == 0 else 1 - c
            for py in (0, 1):
                src = gts.at[feature_rows(px, py, pc)]
                lanes = pl.ds(pl.multiple_of(s * T, T), T)
                if step == 0 and k == 0:
                    gt[py * C : (py + 1) * C, lanes] = src[...]
                else:
                    sends.append(
                        send(
                            src, gt.at[py * C : (py + 1) * C, lanes],
                            t_send.at[step, k, py], t_recv.at[s, py], at(px, y, pc),
                        )
                    )

    inv_n = jnp.broadcast_to(inv, (LANES, T)).T
    pull_n = jnp.broadcast_to(pull, (LANES, T)).T
    for px in range(4):
        for k in range(Q // LANES):
            k0 = px * Q + k * LANES
            row = gall[px, 0:1, k * LANES : (k + 1) * LANES].astype(F32)
            sm = rbuf[:, k0 : k0 + LANES].astype(F32) + ptr[k0 : k0 + LANES, :].T.astype(F32)
            ct = cbuf[:, k0 : k0 + LANES].astype(F32)
            nm = sm * inv_n
            nbuf[:, k0 : k0 + LANES] = (nm * row).astype(BF16)
            gbuf[:, k0 : k0 + LANES] = (ct * row * inv_n - sm * pull_n).astype(BF16)
            pg[px, :, k * LANES : (k + 1) * LANES] = folded(ct * nm)
    store_n = pltpu.make_async_copy(nbuf, normed_out, out_sem.at[0])
    store_g = pltpu.make_async_copy(gbuf, grad_out, out_sem.at[1])
    store_n.start()
    store_g.start()
    for i, k in enumerate((1, 2, 3)):
        px = rx(k)
        sends.append(send(pg.at[px], pgx.at[i], s1_send.at[i], s1_recv.at[i], at(px, y, c)))

    for k in (0, 1):
        for step in range(4):
            if k == 0 and step == 0:
                continue
            px, pc = rx(step), (c if k == 0 else 1 - c)
            for py in (0, 1):
                lanes = pl.ds(pl.multiple_of((px * 2 + pc) * T, T), T)
                got(gt.at[py * C : (py + 1) * C, lanes], t_send.at[step, k, py], t_recv.at[px * 2 + pc, py])

    def ycopy(j):
        return pltpu.make_async_remote_copy(
            src_ref=ysend.at[j], dst_ref=yrecv.at[j], send_sem=y_send.at[j], recv_sem=y_recv.at[j],
            device_id=at(x, 1 - y, c), device_id_type=MESH,
        )

    def zcopy(j):
        return pltpu.make_async_remote_copy(
            src_ref=new.at[j], dst_ref=other.at[j], send_sem=z_send.at[j], recv_sem=z_recv.at[j],
            device_id=at(x, y, c, dst_r), device_id_type=MESH,
        )

    def products(j, _):
        lanes = pl.ds(pl.multiple_of(j * CHUNK, CHUNK), CHUNK)
        ysend[j] = (
            jnp.dot(gt[pl.ds(peer_rows, C), :], a[:, lanes], preferred_element_type=F32) * factor
        ).astype(BF16)
        ycopy(j).start()
        own[j] = jnp.dot(gt[pl.ds(my_rows, C), :], a[:, lanes], preferred_element_type=F32) * factor
        return 0

    lax.fori_loop(0, NCH, products, 0)

    def update(j, _):
        lanes = pl.ds(pl.multiple_of(j * CHUNK, CHUNK), CHUNK)
        ycopy(j).wait()
        grad = own[j] + yrecv[j].astype(F32)
        new[j] = (wt[pl.ds(my_rows, C), lanes].astype(F32) - RATE_WEIGHT * grad).astype(BF16)
        zcopy(j).start()
        return 0

    lax.fori_loop(0, NCH, update, 0)

    for i, k in enumerate((3, 2, 1)):
        got(pgx.at[i], s1_send.at[i], s1_recv.at[i])
    pgs[...] = pg[x] + pgx[0] + pgx[1] + pgx[2]
    for i, peer in enumerate(quad):
        sends.append(send(pgs, pgq.at[i], s2_send.at[i], s2_recv.at[i], peer))
    for i in range(3):
        got(pgq.at[i], s2_send.at[i], s2_recv.at[i])
    gg = (pgs[...] + pgq[0] + pgq[1] + pgq[2]).sum(axis=0, keepdims=True)
    mgain[...] = jnp.broadcast_to(gall[x, 0:1, :].astype(F32) - RATE_GAIN * gg, mgain.shape).astype(BF16)
    window = pl.ds(pl.multiple_of((y * 2 + c) * LANES, LANES), 2 * LANES)
    ngain[...] = mgain[:, window]
    sends.append(send(ngain, ogain, zg_send, zg_recv, at(x, y, c, dst_r)))

    def mix(j, _):
        zcopy(j).wait()
        mixed[j] = (0.5 * (new[j].astype(F32) + other[j].astype(F32))).astype(BF16)
        lanes = pl.ds(pl.multiple_of(j * CHUNK, CHUNK), CHUNK)
        pltpu.make_async_copy(mixed.at[j], mixed_out.at[:, lanes], out_sem.at[2 + j]).start()
        return 0

    lax.fori_loop(0, NCH, mix, 0)
    got(ogain, zg_send, zg_recv)
    mgain[:, 0 : 2 * LANES] = (0.5 * (ngain[...].astype(F32) + ogain[...].astype(F32))).astype(BF16)
    store_m = pltpu.make_async_copy(mgain.at[:, 0 : 2 * LANES], mixed_gain_out, out_sem.at[2 + NCH])
    store_m.start()

    for cp in sends:
        cp.wait_send()
    store_n.wait()
    store_g.wait()
    store_m.wait()
    for j in range(NCH):
        lanes = pl.ds(j * CHUNK, CHUNK)
        pltpu.make_async_copy(mixed.at[j], mixed_out.at[:, lanes], out_sem.at[2 + j]).wait()


def fused(residual, attention, weight, gain_placed, cotangent, level):
    dma = pltpu.SemaphoreType.DMA
    vm = pltpu.VMEM
    scratch = [
        vm((8 * T, D), BF16),
        vm((D, C), BF16),
        vm((2 * C, D), BF16),
        vm((T, D), BF16),
        vm((T, D), BF16),
        vm((D, T), BF16),
        vm((D, T), F32),
        vm((4, 2, 2 * C, T), BF16),
        vm((D, T), BF16),
        vm((D, T), BF16),
        vm((2 * C, 8 * T), BF16),
        vm((T, D), BF16),
        vm((T, D), BF16),
        vm((NCH, C, CHUNK), BF16),
        vm((NCH, C, CHUNK), BF16),
        vm((NCH, C, CHUNK), F32),
        vm((NCH, C, CHUNK), BF16),
        vm((NCH, C, CHUNK), BF16),
        vm((NCH, C, CHUNK), BF16),
        vm((16, Q), BF16),
        vm((4, 16, Q), BF16),
        vm((4, 16, Q), BF16),
        vm((4, 8, Q), F32),
        vm((3, 8, Q), F32),
        vm((8, Q), F32),
        vm((3, 8, Q), F32),
        vm((16, 2 * LANES), BF16),
        vm((16, 2 * LANES), BF16),
        vm((16, Q), BF16),
        dma((5,)), dma((3 + NCH,)),
        dma((3, 2)), dma((3, 2)), dma((7,)), dma((7,)), dma((2,)), dma((2,)),
        dma((3,)), dma((3,)), dma((3,)), dma((3,)),
        dma((4, 2, 2)), dma((8, 2)), dma((4, 2, 2)), dma((8, 2)),
        dma((3,)), dma((3,)), dma((3,)), dma((3,)),
        dma((NCH,)), dma((NCH,)), dma((NCH,)), dma((NCH,)), dma(()), dma(()),
    ]
    hbm = pl.BlockSpec(memory_space=pl.ANY)
    return pl.pallas_call(
        partial(kernel, 2**level),
        out_shape=(
            jax.ShapeDtypeStruct((T, D), BF16),
            jax.ShapeDtypeStruct((T, D), BF16),
            jax.ShapeDtypeStruct((C, D), BF16),
            jax.ShapeDtypeStruct((16, 2 * LANES), BF16),
        ),
        in_specs=[hbm] * 5,
        out_specs=(hbm,) * 4,
        scratch_shapes=scratch,
        compiler_params=pltpu.CompilerParams(
            collective_id=level, has_side_effects=True, vmem_limit_bytes=56 * 2**20
        ),
        cost_estimate=pl.CostEstimate(flops=4 * 1024 * 320 * D, bytes_accessed=8 * 2**20, transcendentals=0),
        name=f"replica_step_{level}",
    )(attention, residual, cotangent, weight, gain_placed)


def body(residual, attention, out_weight, norm_gain, cotangent, step_index):
    f = lax.axis_index("fsdp")
    q = f % 4
    placed = jnp.zeros((Q,), BF16)
    placed = lax.dynamic_update_slice_in_dim(placed, norm_gain[0], q * C, 0)
    placed = jnp.broadcast_to(placed[None], (16, Q))
    hop_count = lax.axis_size("replica").bit_length() - 1
    args = (residual[0], attention[0], out_weight[0], placed, cotangent[0])
    branches = [
        lambda ops, level=level: fused(*ops, level) for level in range(hop_count)
    ]
    normed, grad, mixed_t, gain_window = lax.switch(step_index[0] % hop_count, branches, args)
    mixed_gain = lax.dynamic_slice_in_dim(gain_window[0], q * 32, C, 0)
    return normed[None], grad[None], mixed_t.T[None], mixed_gain[None]


def solution(mesh):
    return jax.shard_map(
        body,
        mesh=mesh,
        in_specs=(
            P("replica", "fsdp", None),
            P("replica", "fsdp", None),
            P("replica", None, "fsdp"),
            P("replica", "fsdp"),
            P("replica", "fsdp", None),
            P(),
        ),
        out_specs=(
            P("replica", "fsdp", None),
            P("replica", "fsdp", None),
            P("replica", None, "fsdp"),
            P("replica", "fsdp"),
        ),
        check_vma=False,
    )
```

time: 341 us -> 121 us (0.35)
  the two profiles are of different devices: /device:TPU:160 before, /device:TPU:1 now
where the time goes in v1:
time: 121 us
  Pallas kernels  112 us (93%)
  local copies, waits for them, and re-layouts  6.42 us (5%)
  between operations  1.33 us (1%)
    pallas_call x1, Pallas kernels, fused(): pl.pallas_call(partial(kernel, 2 ** level), out_shape=(jax.ShapeDtypeStru...  112 us
    unnamed x3, local copies, waits for them, and re-layouts  2.56 us

profile of v1, /device:TPU:1, one launch (start us, length us, event | category | flops | bytes accessed | tf_op | source)
XLA Modules:
  0.0 121.3 jit_solution(10640356315420745155)
XLA Ops:
  1.3 116.8 %conditional.1 = ((bf16[128,2560]{1,0:T(8,128)(2,1)S(1)}, bf16[128,2560]{1,0:T(8,128)(2,1)S(1)}, bf16[160,2560]{1,0:T(8,128)(2,1)S(1)}, bf16[16,256]{1,0:T(8,128)(2,1)S(1)})) conditional(s32[]{:T(128)} %clamp.3, (bf16[1,128,2560]{2,1,0:T(8,128)(2,1)}, bf16[1,128,2560]{2,1,0:T(8,128)(2,1)}, ...), branch_computations={%region_0.1_spmd.clone, %region_1.2_spmd.clone, %region_2.3_spmd.c... | conditional | flops 3355443200 | bytes 15294326 | solution.py:435
  1.3 0.0 copy-start
  1.3 0.0 copy-start.5
  1.4 0.8 reduce
  2.2 0.2 dynamic_update_slice.23
  2.4 0.6 broadcast_in_dim.92.gain
  3.0 2.3 %copy.60 = bf16[1,2560,160]{2,1,0:T(8,128)(2,1)} copy(bf16[1,2560,160]{1,2,0:T(8,128)(2,1)} %get-tuple-element.486) | data formatting | bytes 1638400 | tf_op jit(solution)/shard_map
  5.4 0.0 copy-done
  5.4 0.0 copy-done.5
  5.4 112.5 %replica_step_0.2 = (bf16[128,2560]{1,0:T(8,128)(2,1)S(1)}, bf16[128,2560]{1,0:T(8,128)(2,1)S(1)}, bf16[160,2560]{1,0:T(8,128)(2,1)S(1)}, bf16[16,256]{1,0:T(8,128)(2,1)S(1)}) custom-call(bf16[128,2560]{1,0:T(8,128)(2,1)S(1)} %bitcast.34, bf16[128,2560]{1,0:T(8,128)(2,1)S(1)} %bitcast.39, bf16[128,2560]{1,0:T(8,128)(2,1)} %bitcast.44, ...), custom_call_target="tpu_custom_call" | custom-call | flops 3355443200 | bytes 8388608 | tf_op jit(solution)/shard_map/cond/branch_0_fun/replica_step_0/pallas_call | solution.py:405
  118.1 0.6 constant_dynamic-slice_fusion
  118.7 0.8 copy.94
  119.6 0.8 copy.95
  120.4 0.9 copy.96
  (2 shorter events, 0.0 us)
Async XLA Ops:
  1.3 4.0 %copy-start = (bf16[1,128,2560]{2,1,0:T(8,128)(2,1)S(1)}, bf16[1,128,2560]{2,1,0:T(8,128)(2,1)}, u32[]{:S(2)}) copy-start(bf16[1,128,2560]{2,1,0:T(8,128)(2,1)} %get-tuple-element.408) | copy-start | bytes 1966084 | tf_op jit(solution)/shard_map/cond
  1.3 4.0 %copy-start.5 = (bf16[1,128,2560]{2,1,0:T(8,128)(2,1)S(1)}, bf16[1,128,2560]{2,1,0:T(8,128)(2,1)}, u32[]{:S(2)}) copy-start(bf16[1,128,2560]{2,1,0:T(8,128)(2,1)} %get-tuple-element.409) | copy-start | bytes 1966084 | tf_op jit(solution)/shard_map/cond

commit v2 on v0

v2 whole, which is shorter than its diff:
```python
from functools import partial
import math

import jax
import jax.numpy as jnp
from jax import lax
from jax.experimental import pallas as pl
from jax.experimental.pallas import tpu as pltpu
from jax.sharding import PartitionSpec as P

EPSILON = 1e-05
RATE_WEIGHT = 0.2
RATE_GAIN = 0.005
MESH = pl.DeviceIdType.MESH
F32 = jnp.float32
BF16 = jnp.bfloat16

D = 2560
T = 128
C = 160
Q = 640
LANES = 128
CHUNK = 256
NCH = D // CHUNK
LONGS = {8: 2}


def kernel(
    distance, longs,
    att, res, cot, weight, gain,
    normed_out, grad_out, mixed_out, mixed_gain_out,
    a, wt, rbuf, cbuf, res_t, gn_t, pts, ptr, gts, gt, nbuf, gbuf,
    ysend, yrecv, new, other, mixed,
    gplace, gquad, gall, pg, pgx, pgs, pgq, ngain, ogain,
    load_sem, out_sem,
    a_send, a_recv, sib_send, sib_recv, w_send, w_recv,
    g1_send, g1_recv, g2_send, g2_recv,
    p_send, p_recv, t_send, t_recv, s1_send, s1_recv, s2_send, s2_recv,
    y_send, y_recv, z_send, z_recv, v_send, zg_send, zg_recv,
):
    r = lax.axis_index("replica")
    f = lax.axis_index("fsdp")
    replicas = lax.axis_size("replica")
    x, y, c = f // 4, (f // 2) % 2, f % 2
    s = x * 2 + c
    sib = 1 - c
    factor = 1.0 / math.sqrt(D)

    def at(px, py, pc, pr=r):
        return (pr, px * 4 + py * 2 + pc)

    def rx(step):
        return (x + step) % 4

    def remote(src, dst, ss, rs, target):
        return pltpu.make_async_remote_copy(
            src_ref=src, dst_ref=dst, send_sem=ss, recv_sem=rs, device_id=target, device_id_type=MESH
        )

    sends = []

    def send(src, dst, ss, rs, target):
        cp = remote(src, dst, ss, rs, target)
        cp.start()
        sends.append(cp)

    def got(ref, ss, rs):
        remote(ref, ref, ss, rs, at(rx(1), y, c)).wait_recv()

    def rows(slot, start=0, size=T):
        return pl.ds(pl.multiple_of(slot * T + start, 64), size)

    my_rows = pl.multiple_of(y * C, 32)
    peer_rows = pl.multiple_of((1 - y) * C, 32)

    def columns(py, pc, start=0, size=C):
        return pl.ds(pl.multiple_of((py * 2 + pc) * C + start, 16), size)

    load_a = pltpu.make_async_copy(att, a.at[rows(s)], load_sem.at[0])
    load_w = pltpu.make_async_copy(weight, wt.at[columns(y, c)], load_sem.at[1])
    load_r = pltpu.make_async_copy(res, rbuf, load_sem.at[2])
    load_c = pltpu.make_async_copy(cot, cbuf, load_sem.at[3])
    for cp in (load_a, load_w, load_r, load_c):
        cp.start()

    leg = (replicas - distance) // 2
    dst_r = (r + distance) % replicas
    src_r = (r + replicas - distance) % replicas
    via_r = (r + replicas - leg) % replicas
    peers = [at(rx(k), y, c) for k in (1, 2, 3)] + [at(rx(k), y, sib) for k in range(4)]
    peers += [at(x, 1 - y, c), at(x, 1 - y, sib), at(x, y, c, dst_r)]
    if 2 * distance != replicas:
        peers.append(at(x, y, c, src_r))
    if longs:
        peers += [at(x, y, c, via_r), at(x, y, c, (r + leg) % replicas)]
    barrier = pltpu.get_barrier_semaphore()
    for peer in peers:
        pl.semaphore_signal(barrier, inc=1, device_id=peer, device_id_type=MESH)

    gplace[...] = jnp.zeros(gplace.shape, F32)
    gplace[:, 0:C] = jnp.broadcast_to(gain[...].astype(F32), (8, C))
    gplace[...] = pltpu.roll(gplace[...], (y * 2 + c) * C, 1)
    gquad[0] = gplace[...]
    load_a.wait()
    load_w.wait()
    pl.semaphore_wait(barrier, len(peers))

    quad = [at(x, y, sib), at(x, 1 - y, c), at(x, 1 - y, sib)]
    for i, peer in enumerate(quad):
        send(gplace, gquad.at[1 + i], g1_send.at[i], g1_recv.at[i], peer)

    left, right, far = rx(3), rx(1), rx(2)
    for h in (0, 1):
        span = rows(s, 64 * h, 64)
        send(a.at[span], a.at[span], a_send.at[0, h], a_recv.at[0, h], at(right, y, c))
        h2 = 1 - h
        span = rows(s, 64 * h2, 64)
        send(a.at[span], a.at[span], a_send.at[1, h2], a_recv.at[1, h2], at(left, y, c))
    for h in (0, 1):
        span = columns(y, c, 80 * h, 80)
        send(wt.at[span], wt.at[span], w_send.at[h], w_recv.at[h], at(x, 1 - y, c))
    send(wt.at[columns(y, c)], wt.at[columns(y, c)], w_send.at[2], w_recv.at[2], at(x, y, sib))
    send(a.at[rows(s)], a.at[rows(s)], sib_send.at[0], sib_recv.at[0], at(x, y, sib))

    load_r.wait()
    load_c.wait()

    def turn_res(k, _):
        k0 = pl.multiple_of(k * LANES, LANES)
        res_t[pl.ds(k0, LANES), :] = rbuf[:, pl.ds(k0, LANES)].T
        return 0

    lax.fori_loop(0, D // LANES, turn_res, 0)

    for i in range(3):
        got(gquad.at[1 + i], g1_send.at[i], g1_recv.at[i])
    gall[x] = gquad[0] + gquad[1] + gquad[2] + gquad[3]
    for i, k in enumerate((1, 2, 3)):
        send(gall.at[x], gall.at[x], g2_send.at[i], g2_recv.at[i], at(rx(k), y, c))

    def projected(px, py):
        start = pl.multiple_of(py * 2 * C, 64)
        width = 512

        def part(k, total):
            depth = pl.ds(pl.multiple_of(k * width, width), width)
            return total + lax.dot_general(
                wt[pl.ds(start, 2 * C), depth], a[rows(px * 2 + c), depth], (((1,), (1,)), ((), ())),
                preferred_element_type=F32,
            )

        out = lax.fori_loop(0, D // width, part, jnp.zeros((2 * C, T), F32))
        pts[px, pl.ds(start, 2 * C), :] = (out * factor).astype(BF16)

    def feature_rows(px, py, pc):
        return pl.ds(pl.multiple_of(px * Q + py * 2 * C + pc * C, 32), C)

    def half_rows(px, py):
        return pl.ds(pl.multiple_of(px * Q + py * 2 * C, 64), 2 * C)

    def hand_out(step, px, i):
        py = y if i == 0 else 1 - y
        src = pts.at[px, pl.ds(pl.multiple_of(py * 2 * C, 64), 2 * C)]
        span = half_rows(x, py)
        if step == 0:
            ptr[span, :] = src[...]
        else:
            send(src, ptr.at[span], p_send.at[step, i], p_recv.at[x, i], at(px, y, c))

    def forward(slot, h, i):
        span = rows(slot, 64 * h, 64)
        send(a.at[span], a.at[span], sib_send.at[i], sib_recv.at[i], at(x, y, sib))

    def pass_on(slot, h, target):
        span = rows(slot, 64 * h, 64)
        send(a.at[span], a.at[span], a_send.at[2, h], a_recv.at[2, h], target)

    got(wt.at[columns(y, sib)], w_send.at[2], w_recv.at[2])
    projected(x, y)
    hand_out(0, x, 0)

    left_c, right_c, far_c = left * 2 + c, right * 2 + c, far * 2 + c
    got(a.at[rows(left_c, 0, 64)], a_send.at[0, 0], a_recv.at[0, 0])
    pass_on(left_c, 0, at(right, y, c))
    got(a.at[rows(right_c, 64, 64)], a_send.at[1, 1], a_recv.at[1, 1])
    pass_on(right_c, 1, at(left, y, c))
    forward(left_c, 0, 1)
    forward(right_c, 1, 4)
    got(a.at[rows(left_c, 64, 64)], a_send.at[0, 1], a_recv.at[0, 1])
    forward(left_c, 1, 2)
    got(a.at[rows(right_c, 0, 64)], a_send.at[1, 0], a_recv.at[1, 0])
    forward(right_c, 0, 3)

    for i, k in enumerate((3, 2, 1)):
        got(gall.at[rx(k)], g2_send.at[i], g2_recv.at[i])
    def turn_cot(n, _):
        span = pl.ds(pl.multiple_of(n * LANES, LANES), LANES)
        row = gall[n // 5, 0:1, pl.ds(pl.multiple_of(n % 5 * LANES, LANES), LANES)]
        gn_t[span, :] = (cbuf[:, span].astype(F32) * row).T
        return 0

    lax.fori_loop(0, D // LANES, turn_cot, 0)

    def near(n, _):
        projected((x + 3 + 2 * n) % 4, y)
        return 0

    lax.fori_loop(0, 2, near, 0)
    hand_out(3, left, 0)
    hand_out(1, right, 0)

    for h in (0, 1):
        span = columns(1 - y, c, 80 * h, 80)
        got(wt.at[span], w_send.at[h], w_recv.at[h])
        send(wt.at[span], wt.at[span], w_send.at[3 + h], w_recv.at[3 + h], at(x, y, sib))
    for h in (0, 1):
        got(wt.at[columns(1 - y, sib, 80 * h, 80)], w_send.at[3 + h], w_recv.at[3 + h])

    def near_again(n, _):
        projected((x + 3 + n) % 4, 1 - y)
        return 0

    lax.fori_loop(0, 3, near_again, 0)
    hand_out(3, left, 1)
    hand_out(1, right, 1)
    hand_out(0, x, 1)
    for h in (0, 1):
        got(a.at[rows(far_c, 64 * h, 64)], a_send.at[2, h], a_recv.at[2, h])

    def last(n, _):
        projected(far, (y + n) % 2)
        return 0

    lax.fori_loop(0, 2, last, 0)
    hand_out(2, far, 0)
    hand_out(2, far, 1)
    for h in (0, 1):
        forward(far_c, h, 5 + h)

    for step in (3, 1, 2):
        for i in (0, 1):
            px, py = rx(step), (y if i == 0 else 1 - y)
            got(ptr.at[half_rows(px, py)], p_send.at[step, i], p_recv.at[px, i])

    def folded(v):
        return v.reshape(LANES // 8, 8, T).sum(axis=0)

    def stats(k, carry):
        ss, gs = carry
        span = pl.ds(pl.multiple_of(k * LANES, LANES), LANES)
        sm = res_t[span, :].astype(F32) + ptr[span, :].astype(F32)
        return ss + folded(sm * sm), gs + folded(sm * gn_t[span, :])

    zero = jnp.zeros((8, T), F32)
    ss, gs = lax.fori_loop(0, D // LANES, stats, (zero, zero))
    inv = lax.rsqrt(ss.sum(axis=0, keepdims=True) * (1.0 / D) + EPSILON)
    inner = gs.sum(axis=0, keepdims=True) * (1.0 / D) * inv
    pull = inner * inv * inv

    my_lanes = pl.ds(pl.multiple_of(s * T, T), T)

    def gradient_copy(n):
        m = n % 8
        px, pc = (x + 2 + m // 2) % 4, (c + m) % 2
        py = (y + 1 + n // 8) % 2
        span = feature_rows(px, py, pc)
        land = pl.ds(pl.multiple_of(py * C, 32), C)
        cp = remote(
            gts.at[span], gt.at[land, my_lanes], t_send.at[n], t_recv.at[s, n // 8], at(px, y, pc)
        )
        return cp, span, land, m == 4

    def gradients(n, _):
        cp, span, land, mine = gradient_copy(n)
        sm = res_t[span, :].astype(F32) + ptr[span, :].astype(F32)
        gts[span, :] = (gn_t[span, :] * inv - sm * pull).astype(BF16)

        @pl.when(mine)
        def _():
            gt[land, my_lanes] = gts[span, :]

        @pl.when(jnp.logical_not(mine))
        def _():
            cp.start()

        return 0

    lax.fori_loop(0, 16, gradients, 0)

    def got_gradients(i):
        land = pl.ds(my_rows if i else peer_rows, C)
        for k in (0, 1):
            for step in range(4):
                if k == 0 and step == 0:
                    continue
                slot = rx(step) * 2 + (c if k == 0 else sib)
                lanes = pl.ds(pl.multiple_of(slot * T, T), T)
                got(gt.at[land, lanes], t_send.at[0], t_recv.at[slot, i])

    def chunk(j):
        return pl.ds(pl.multiple_of(j * CHUNK, CHUNK), CHUNK)

    def ycopy(j):
        return remote(ysend.at[j], yrecv.at[j], y_send.at[j], y_recv.at[j], at(x, 1 - y, c))

    def theirs(j, _):
        part = jnp.dot(gt[pl.ds(peer_rows, C), :], a[:, chunk(j)], preferred_element_type=F32)
        ysend[j] = (part * factor).astype(BF16)
        ycopy(j).start()
        return 0

    inv_n = jnp.broadcast_to(inv, (LANES, T)).T
    pull_n = jnp.broadcast_to(pull, (LANES, T)).T

    def token_rows(px):
        def part(k, _):
            span = pl.ds(pl.multiple_of(px * Q + k * LANES, LANES), LANES)
            within = pl.ds(pl.multiple_of(k * LANES, LANES), LANES)
            row = gall[px, 0:1, within]
            sm = rbuf[:, span].astype(F32) + ptr[span, :].T.astype(F32)
            ct = cbuf[:, span].astype(F32)
            nm = sm * inv_n
            nbuf[:, span] = (nm * row).astype(BF16)
            gbuf[:, span] = (ct * row * inv_n - sm * pull_n).astype(BF16)
            pg[px, :, within] = folded(ct * nm)
            return 0

        lax.fori_loop(0, Q // LANES, part, 0)

    store_n = pltpu.make_async_copy(nbuf, normed_out, out_sem.at[0])
    store_g = pltpu.make_async_copy(gbuf, grad_out, out_sem.at[1])

    def gain_sums():
        store_n.start()
        store_g.start()
        for i, k in enumerate((1, 2, 3)):
            px = rx(k)
            send(pg.at[px], pgx.at[i], s1_send.at[i], s1_recv.at[i], at(px, y, c))

    def gain_quad():
        for i, k in enumerate((3, 2, 1)):
            got(pgx.at[i], s1_send.at[i], s1_recv.at[i])
        pgs[...] = pg[x] + pgx[0] + pgx[1] + pgx[2]
        for i, peer in enumerate(quad):
            send(pgs, pgq.at[i], s2_send.at[i], s2_recv.at[i], peer)

    def gain_new():
        for i in range(3):
            got(pgq.at[i], s2_send.at[i], s2_recv.at[i])
        gg = (pgs[...] + pgq[0] + pgq[1] + pgq[2]).sum(axis=0, keepdims=True)
        gquad[0] = jnp.broadcast_to(gall[x, 0:1, :] - RATE_GAIN * gg, gplace.shape)
        window = pl.ds(pl.multiple_of((y * 2 + c) * LANES, LANES), 2 * LANES)
        ngain[...] = gquad[0, :, window].astype(BF16).astype(F32)
        send(ngain, ogain, zg_send, zg_recv, at(x, y, c, dst_r))

    got(a.at[rows(x * 2 + sib)], sib_send.at[0], sib_recv.at[0])
    for px, base in ((left, 1), (right, 3), (far, 5)):
        for h in (0, 1):
            got(a.at[rows(px * 2 + sib, 64 * h, 64)], sib_send.at[base + h], sib_recv.at[base + h])
    got_gradients(0)
    lax.fori_loop(0, NCH, theirs, 0)
    got_gradients(1)

    def zcopy(j):
        slot, target = j, dst_r
        if longs:
            early = j % 2 * (j < 2 * longs)
            slot = j + early * (NCH + j // 2 - j)
            target = dst_r + early * (via_r - dst_r)
        return remote(new.at[j], other.at[slot], z_send.at[j], z_recv.at[slot], at(x, y, c, target))

    def update(j):
        part = jnp.dot(gt[pl.ds(my_rows, C), :], a[:, chunk(j)], preferred_element_type=F32)
        ycopy(j).wait()
        grad = part * factor + yrecv[j].astype(F32)
        new[j] = (wt[columns(y, c), chunk(j)].astype(F32) - RATE_WEIGHT * grad).astype(BF16)
        zcopy(j).start()

    def update_beside(j, _):
        update(j)
        token_rows(j)
        return 0

    def update_alone(j, _):
        update(j)
        return 0

    lax.fori_loop(0, 4, update_beside, 0)
    gain_sums()
    lax.fori_loop(4, 7, update_alone, 0)
    gain_quad()
    lax.fori_loop(7, NCH, update_alone, 0)
    gain_new()

    for i in range(longs):
        got(other.at[NCH + i], z_send.at[0], z_recv.at[NCH + i])
        j = 2 * i + 1
        send(other.at[NCH + i], other.at[j], v_send.at[i], z_recv.at[j], at(x, y, c, via_r))

    def store_mixed(j):
        return pltpu.make_async_copy(mixed.at[j], mixed_out.at[:, chunk(j)], out_sem.at[2 + j])

    def mix(n, _):
        j = (n + 4) % NCH
        got(other.at[j], z_send.at[0], z_recv.at[j])
        mixed[j] = (0.5 * (new[j].astype(F32) + other[j].astype(F32))).astype(BF16)
        store_mixed(j).start()
        return 0

    lax.fori_loop(0, NCH, mix, 0)
    got(ogain, zg_send, zg_recv)
    mean = 0.5 * (ngain[...] + ogain[...])
    turned = pltpu.roll(mean, (2 * LANES - (y * 2 + c) * 32) % (2 * LANES), 1)
    mixed_gain_out[...] = turned[0:1, 0:C].astype(BF16)

    def sent(n, _):
        cp, _, _, mine = gradient_copy(n)

        @pl.when(jnp.logical_not(mine))
        def _():
            cp.wait_send()

        return 0

    lax.fori_loop(0, 16, sent, 0)

    def finished(j, _):
        zcopy(j).wait_send()
        store_mixed(j).wait()
        return 0

    lax.fori_loop(0, NCH, finished, 0)
    store_n.wait()
    store_g.wait()
    for cp in sends:
        cp.wait_send()


def fused(residual, attention, weight, gain, cotangent, level):
    longs = LONGS.get(2**level, 0)
    dma = pltpu.SemaphoreType.DMA
    vm = pltpu.VMEM
    scratch = [
        vm((8 * T, D), BF16),
        vm((Q, D), BF16),
        vm((T, D), BF16),
        vm((T, D), BF16),
        vm((D, T), BF16),
        vm((D, T), F32),
        vm((4, Q, T), BF16),
        vm((D, T), BF16),
        vm((D, T), BF16),
        vm((2 * C, 8 * T), BF16),
        vm((T, D), BF16),
        vm((T, D), BF16),
        vm((NCH, C, CHUNK), BF16),
        vm((NCH, C, CHUNK), BF16),
        vm((NCH, C, CHUNK), BF16),
        vm((NCH + longs, C, CHUNK), BF16),
        vm((NCH, C, CHUNK), BF16),
        vm((8, Q), F32),
        vm((4, 8, Q), F32),
        vm((4, 8, Q), F32),
        vm((4, 8, Q), F32),
        vm((3, 8, Q), F32),
        vm((8, Q), F32),
        vm((3, 8, Q), F32),
        vm((8, 2 * LANES), F32),
        vm((8, 2 * LANES), F32),
        dma((4,)), dma((2 + NCH,)),
        dma((3, 2)), dma((3, 2)), dma((7,)), dma((7,)), dma((5,)), dma((5,)),
        dma((3,)), dma((3,)), dma((3,)), dma((3,)),
        dma((4, 2)), dma((4, 2)), dma((16,)), dma((8, 2)),
        dma((3,)), dma((3,)), dma((3,)), dma((3,)),
        dma((NCH,)), dma((NCH,)), dma((NCH,)), dma((NCH + longs,)),
        dma((max(longs, 1),)), dma(()), dma(()),
    ]
    hbm = pl.BlockSpec(memory_space=pl.ANY)
    vmem = pl.BlockSpec(memory_space=pltpu.VMEM)
    return pl.pallas_call(
        partial(kernel, 2**level, longs),
        out_shape=(
            jax.ShapeDtypeStruct((T, D), BF16),
            jax.ShapeDtypeStruct((T, D), BF16),
            jax.ShapeDtypeStruct((C, D), BF16),
            jax.ShapeDtypeStruct((1, C), BF16),
        ),
        in_specs=[hbm] * 4 + [vmem],
        out_specs=(hbm, hbm, hbm, vmem),
        scratch_shapes=scratch,
        compiler_params=pltpu.CompilerParams(
            collective_id=level, has_side_effects=True, vmem_limit_bytes=56 * 2**20
        ),
        cost_estimate=pl.CostEstimate(flops=4 * 1024 * 320 * D, bytes_accessed=8 * 2**20, transcendentals=0),
        name=f"replica_step_{level}",
    )(attention, residual, cotangent, weight, gain)


def body(residual, attention, out_weight, norm_gain, cotangent, step_index):
    hop_count = lax.axis_size("replica").bit_length() - 1
    args = (residual[0], attention[0], out_weight[0].T, norm_gain, cotangent[0])
    branches = [lambda ops, level=level: fused(*ops, level) for level in range(hop_count)]
    normed, grad, mixed_t, mixed_gain = lax.switch(step_index[0] % hop_count, branches, args)
    return normed[None], grad[None], mixed_t.T[None], mixed_gain


def solution(mesh):
    return jax.shard_map(
        body,
        mesh=mesh,
        in_specs=(
            P("replica", "fsdp", None),
            P("replica", "fsdp", None),
            P("replica", None, "fsdp"),
            P("replica", "fsdp"),
            P("replica", "fsdp", None),
            P(),
        ),
        out_specs=(
            P("replica", "fsdp", None),
            P("replica", "fsdp", None),
            P("replica", None, "fsdp"),
            P("replica", "fsdp"),
        ),
        check_vma=False,
    )
```

time: 341 us -> 127 us (0.37)
  the two profiles are of different devices: /device:TPU:160 before, /device:TPU:42 now
where the time goes in v2:
time: 127 us; the launch traced here: 126 us
  Pallas kernels  121 us (95%)
  local copies, waits for them, and re-layouts  3.8 us (3%)
  between operations  1.31 us (1%)
    pallas_call x1, Pallas kernels, fused(): pl.pallas_call(partial(kernel, 2 ** level, longs), out_shape=(jax.ShapeDt...  121 us
    unnamed x6, local copies, waits for them, and re-layouts  3.8 us

profile of v2, /device:TPU:42, one launch (start us, length us, event | category | flops | bytes accessed | tf_op | source)
XLA Modules:
  0.0 126.4 jit_solution(4078297123269021409)
XLA Ops:
  1.3 0.0 copy-start
  1.3 0.7 copy-done
  2.0 121.3 %conditional.1 = ((bf16[128,2560]{1,0:T(8,128)(2,1)S(1)}, bf16[128,2560]{1,0:T(8,128)(2,1)S(1)}, bf16[160,2560]{1,0:T(8,128)(2,1)S(1)}, bf16[1,160]{1,0:T(2,128)(2,1)S(1)})) conditional(s32[]{:T(128)} %clamp.3, (bf16[1,128,2560]{2,1,0:T(8,128)(2,1)}, bf16[1,128,2560]{2,1,0:T(8,128)(2,1)}, ...), branch_computations={%region_0.1_spmd, %region_1.2_spmd, %region_2.3_spmd, %region_3.4_... | conditional | flops 3355443200 | bytes 8388616 | solution.py:503
  2.0 121.2 %replica_step_3.1 = (bf16[128,2560]{1,0:T(8,128)(2,1)S(1)}, bf16[128,2560]{1,0:T(8,128)(2,1)S(1)}, bf16[160,2560]{1,0:T(8,128)(2,1)S(1)}, bf16[1,160]{1,0:T(2,128)(2,1)S(1)}) custom-call(bf16[128,2560]{1,0:T(8,128)(2,1)} %bitcast.35, bf16[128,2560]{1,0:T(8,128)(2,1)} %bitcast.40, bf16[128,2560]{1,0:T(8,128)(2,1)} %bitcast.45, ...), custom_call_target="tpu_custom_call" | custom-call | flops 3355443200 | bytes 8388608 | tf_op jit(solution)/shard_map/cond/branch_3_fun/replica_step_3/pallas_call | solution.py:480
  123.2 0.8 copy.55
  124.1 0.8 copy.56
  124.9 0.9 copy.57
  125.8 0.6 copy.58
Async XLA Ops:
  1.3 0.7 copy-start

commit v3 on v2

--- a/solution.py
+++ b/solution.py
@@ -29,7 +29,7 @@
     distance, longs,
     att, res, cot, weight, gain,
     normed_out, grad_out, mixed_out, mixed_gain_out,
-    a, wt, rbuf, cbuf, res_t, gn_t, pts, ptr, gts, gt, nbuf, gbuf,
+    gain_in, a, wt, rbuf, cbuf, res_t, gn_t, pts, ptr, gts, gt, nbuf, gbuf,
     ysend, yrecv, new, other, mixed,
     gplace, gquad, gall, pg, pgx, pgs, pgq, ngain, ogain,
     load_sem, out_sem,
@@ -80,7 +80,8 @@
     load_w = pltpu.make_async_copy(weight, wt.at[columns(y, c)], load_sem.at[1])
     load_r = pltpu.make_async_copy(res, rbuf, load_sem.at[2])
     load_c = pltpu.make_async_copy(cot, cbuf, load_sem.at[3])
-    for cp in (load_a, load_w, load_r, load_c):
+    load_g = pltpu.make_async_copy(gain, gain_in, load_sem.at[4])
+    for cp in (load_g, load_a, load_w, load_r, load_c):
         cp.start()
 
     leg = (replicas - distance) // 2
@@ -98,7 +99,8 @@
         pl.semaphore_signal(barrier, inc=1, device_id=peer, device_id_type=MESH)
 
     gplace[...] = jnp.zeros(gplace.shape, F32)
-    gplace[:, 0:C] = jnp.broadcast_to(gain[...].astype(F32), (8, C))
+    load_g.wait()
+    gplace[:, 0:C] = jnp.broadcast_to(gain_in[...].astype(F32), (8, C))
     gplace[...] = pltpu.roll(gplace[...], (y * 2 + c) * C, 1)
     gquad[0] = gplace[...]
     load_a.wait()
@@ -140,16 +142,10 @@
 
     def projected(px, py):
         start = pl.multiple_of(py * 2 * C, 64)
-        width = 512
-
-        def part(k, total):
-            depth = pl.ds(pl.multiple_of(k * width, width), width)
-            return total + lax.dot_general(
-                wt[pl.ds(start, 2 * C), depth], a[rows(px * 2 + c), depth], (((1,), (1,)), ((), ())),
-                preferred_element_type=F32,
-            )
-
-        out = lax.fori_loop(0, D // width, part, jnp.zeros((2 * C, T), F32))
+        out = lax.dot_general(
+            wt[pl.ds(start, 2 * C), :], a[rows(px * 2 + c), :], (((1,), (1,)), ((), ())),
+            preferred_element_type=F32,
+        )
         pts[px, pl.ds(start, 2 * C), :] = (out * factor).astype(BF16)
 
     def feature_rows(px, py, pc):
@@ -227,32 +223,33 @@
     for h in (0, 1):
         got(a.at[rows(far_c, 64 * h, 64)], a_send.at[2, h], a_recv.at[2, h])
 
-    def last(n, _):
-        projected(far, (y + n) % 2)
-        return 0
-
-    lax.fori_loop(0, 2, last, 0)
+    projected(far, y)
     hand_out(2, far, 0)
+    projected(far, 1 - y)
     hand_out(2, far, 1)
     for h in (0, 1):
         forward(far_c, h, 5 + h)
 
-    for step in (3, 1, 2):
+    def folded(v):
+        return v.reshape(LANES // 8, 8, T).sum(axis=0)
+
+    def stats(n, carry):
+        ss, gs = carry
+        span = pl.ds(pl.multiple_of((x + 3 + n // 5) % 4 * Q + n % 5 * LANES, LANES), LANES)
+        sm = res_t[span, :].astype(F32) + ptr[span, :].astype(F32)
+        return ss + folded(sm * sm), gs + folded(sm * gn_t[span, :])
+
+    def got_features(step):
         for i in (0, 1):
             px, py = rx(step), (y if i == 0 else 1 - y)
             got(ptr.at[half_rows(px, py)], p_send.at[step, i], p_recv.at[px, i])
 
-    def folded(v):
-        return v.reshape(LANES // 8, 8, T).sum(axis=0)
-
-    def stats(k, carry):
-        ss, gs = carry
-        span = pl.ds(pl.multiple_of(k * LANES, LANES), LANES)
-        sm = res_t[span, :].astype(F32) + ptr[span, :].astype(F32)
-        return ss + folded(sm * sm), gs + folded(sm * gn_t[span, :])
-
     zero = jnp.zeros((8, T), F32)
-    ss, gs = lax.fori_loop(0, D // LANES, stats, (zero, zero))
+    got_features(3)
+    got_features(1)
+    sums = lax.fori_loop(0, 15, stats, (zero, zero))
+    got_features(2)
+    ss, gs = lax.fori_loop(15, 20, stats, sums)
     inv = lax.rsqrt(ss.sum(axis=0, keepdims=True) * (1.0 / D) + EPSILON)
     inner = gs.sum(axis=0, keepdims=True) * (1.0 / D) * inv
     pull = inner * inv * inv
@@ -441,6 +438,7 @@
     dma = pltpu.SemaphoreType.DMA
     vm = pltpu.VMEM
     scratch = [
+        vm((1, C), BF16),
         vm((8 * T, D), BF16),
         vm((Q, D), BF16),
         vm((T, D), BF16),
@@ -467,7 +465,7 @@
         vm((3, 8, Q), F32),
         vm((8, 2 * LANES), F32),
         vm((8, 2 * LANES), F32),
-        dma((4,)), dma((2 + NCH,)),
+        dma((5,)), dma((2 + NCH,)),
         dma((3, 2)), dma((3, 2)), dma((7,)), dma((7,)), dma((5,)), dma((5,)),
         dma((3,)), dma((3,)), dma((3,)), dma((3,)),
         dma((4, 2)), dma((4, 2)), dma((16,)), dma((8, 2)),
@@ -485,7 +483,7 @@
             jax.ShapeDtypeStruct((C, D), BF16),
             jax.ShapeDtypeStruct((1, C), BF16),
         ),
-        in_specs=[hbm] * 4 + [vmem],
+        in_specs=[pl.BlockSpec(memory_space=pltpu.HBM)] * 5,
         out_specs=(hbm, hbm, hbm, vmem),
         scratch_shapes=scratch,
         compiler_params=pltpu.CompilerParams(
@@ -496,11 +494,37 @@
     )(attention, residual, cotangent, weight, gain)
 
 
+def hand_over(*refs):
+    *pairs, sems = refs
+    half = len(pairs) // 2
+    copies = [
+        pltpu.make_async_copy(src, dst, sems.at[i])
+        for i, (src, dst) in enumerate(zip(pairs[:half], pairs[half:]))
+    ]
+    for cp in copies:
+        cp.start()
+    for cp in copies:
+        cp.wait()
+
+
+def in_place(*results):
+    anywhere = pl.BlockSpec(memory_space=pl.ANY)
+    return pl.pallas_call(
+        hand_over,
+        out_shape=tuple(jax.ShapeDtypeStruct(v.shape, v.dtype) for v in results),
+        in_specs=[anywhere] * len(results),
+        out_specs=(pl.BlockSpec(memory_space=pltpu.HBM),) * len(results),
+        scratch_shapes=[pltpu.SemaphoreType.DMA((len(results),))],
+        name="hand_over",
+    )(*results)
+
+
 def body(residual, attention, out_weight, norm_gain, cotangent, step_index):
     hop_count = lax.axis_size("replica").bit_length() - 1
     args = (residual[0], attention[0], out_weight[0].T, norm_gain, cotangent[0])
     branches = [lambda ops, level=level: fused(*ops, level) for level in range(hop_count)]
     normed, grad, mixed_t, mixed_gain = lax.switch(step_index[0] % hop_count, branches, args)
+    normed, grad, mixed_t, mixed_gain = in_place(normed, grad, mixed_t, mixed_gain)
     return normed[None], grad[None], mixed_t.T[None], mixed_gain
 
 

time: 127 us -> 123 us (0.969)
  the two profiles are of different devices: /device:TPU:42 before, /device:TPU:1 now
where the time goes in v3:
time: 123 us; the launch traced here: 121 us
  Pallas kernels  119 us (97%)
  between operations  1.49 us (1%)
    pallas_call x1, Pallas kernels, fused(): pl.pallas_call(partial(kernel, 2 ** level, longs), out_shape=(jax.ShapeDt...  117 us

profile of v3, /device:TPU:1, one launch (start us, length us, event | category | flops | bytes accessed | tf_op | source)
XLA Modules:
  0.0 121.0 jit_solution(2489338354559267199)
XLA Ops:
  1.3 0.0 copy-start
  1.3 0.7 copy-done
  2.0 117.4 %conditional.1 = ((bf16[128,2560]{1,0:T(8,128)(2,1)S(1)}, bf16[128,2560]{1,0:T(8,128)(2,1)S(1)}, bf16[160,2560]{1,0:T(8,128)(2,1)S(1)}, bf16[1,160]{1,0:T(2,128)(2,1)S(1)})) conditional(s32[]{:T(128)} %clamp.3, (bf16[128,2560]{1,0:T(8,128)(2,1)}, bf16[128,2560]{1,0:T(8,128)(2,1)}, bf16[128,2560]{1,0:T(8,128)(2,1)}, ...), branch_computations={%region_0.1_spmd, %region_1.2_spmd, %region_2.3_spmd, %region_3.4_... | conditional | flops 3355443200 | bytes 8388616 | solution.py:526
  2.0 117.2 %replica_step_3.1 = (bf16[128,2560]{1,0:T(8,128)(2,1)S(1)}, bf16[128,2560]{1,0:T(8,128)(2,1)S(1)}, bf16[160,2560]{1,0:T(8,128)(2,1)S(1)}, bf16[1,160]{1,0:T(2,128)(2,1)S(1)}) custom-call(bf16[128,2560]{1,0:T(8,128)(2,1)} %get-tuple-element.65.att, bf16[128,2560]{1,0:T(8,128)(2,1)} %get-tuple-element.66.res, bf16[128,2560]{1,0:T(8,128)(2,1)} %get-tuple-element.67.cot, ...), custom_call_target="tpu_custom_call" | custom-call | flops 3355443200 | bytes 8388608 | tf_op jit(solution)/shard_map/cond/branch_3_fun/replica_step_3/pallas_call | solution.py:478
  119.4 1.4 %hand_over.1 = (bf16[128,2560]{1,0:T(8,128)(2,1)}, bf16[128,2560]{1,0:T(8,128)(2,1)}, bf16[160,2560]{1,0:T(8,128)(2,1)}, bf16[1,160]{1,0:T(2,128)(2,1)}) custom-call(bf16[128,2560]{1,0:T(8,128)(2,1)S(1)} %get-tuple-element.87.refs_0_, bf16[128,2560]{1,0:T(8,128)(2,1)S(1)} %get-tuple-element.88.refs_1_, bf16[160,2560]{1,0:T(8,128)(2,1)S(1)} %get-tuple-element.89.refs_2_, ...), custom_call_target="tpu_custom_call" | custom-call | tf_op jit(solution)/shard_map/hand_over/pallas_call | solution.py:512
Async XLA Ops:
  1.3 0.7 copy-start
